TPU v7x, 32 devices: a whole 2x2x4 slice. The times are simulated.
32 devices in a mesh: group: 2 (over x), chan: 8 (over z, y), tm: 2 (over core).
Axes of the slice: x: 2, y: 2, z: 4, core: 2. Of those that a mesh axis runs over, the one named last changes fastest.
Arguments:
- signal: float32 [1664, 16384], P(('group', 'chan'), 'tm'), parts along dimension 0, may hold values from -56 to 56
- valid_flags: int32 [1664, 16], P(('group', 'chan'), 'tm'), parts along dimension 0, may hold values 0 or 1
Outputs:
- correlations: bfloat16 [2, 104, 1664, 512], P(None, 'tm', ('group', 'chan')), parts along dimension 2
There are 2 independent parts, one for each index of `group`. A program takes and returns all parts, laid end to end along the dimension named above; each array names one. Nothing has to cross between parts.
All inputs are finite; a program needn't handle non-finite values. No bound on the sum of `valid_flags` on one device may be relied on, other than what follows from the above.
Results may differ from a plain program's by a relative error of at most 0.009.
Values may be sent and summed in bfloat16 or wider, within the bound.
A program may use at most 192 MiB of HBM per device.

v0:
```python
import functools

import jax
import jax.numpy as jnp
import numpy as np
from jax import lax
from jax.experimental import pallas as pl
from jax.experimental.pallas import tpu as pltpu
from jax.sharding import PartitionSpec as P

WINDOW = 1024
LAGS = 512
ROUNDS = 2
EPSILON = 1e-06
GROUP = 8
LANES = 128
VMEM_LIMIT = 56 * 1024 * 1024


def taper_table(window):
    t = np.arange(window, dtype=np.float32)
    return (0.5 - 0.5 * np.cos(2.0 * np.pi * t / window)).astype(np.float32)[None, :]


def forward_table(window):
    bins = window // 2
    f = np.arange(bins, dtype=np.int64)[:, None]
    t = np.arange(window, dtype=np.int64)[None, :]
    phases = 2.0 * np.pi / window * (f * t % window)
    table = np.stack([np.cos(phases), -np.sin(phases)])
    table = table.reshape(2, bins // GROUP, GROUP, window).transpose(1, 0, 2, 3)
    return table.reshape(window, window).astype(jnp.bfloat16)


def lag_table(window, lag_count, windows):
    f = np.arange(window // 2, dtype=np.int64)[:, None]
    tau = np.arange(lag_count, dtype=np.int64)[None, :] - lag_count // 2
    phases = 2.0 * np.pi / window * (f * tau % window)
    weight = np.where(f == 0, 1.0, 2.0) / (window * float(window * windows) ** 0.5)
    return np.concatenate([weight * np.cos(phases), -weight * np.sin(phases)]).astype(jnp.bfloat16)


def spectra_kernel(signal_ref, flags_ref, taper_ref, table_ref, out_ref, tapered):
    rows = signal_ref.shape[0]
    windows = flags_ref.shape[1]
    groups = out_ref.shape[0]
    flags = flags_ref[...].astype(jnp.float32)
    tapered[...] = jnp.zeros_like(tapered)
    for w in range(windows):
        piece = signal_ref[:, w * WINDOW : (w + 1) * WINDOW]
        scale = lax.rsqrt(jnp.mean(piece * piece, axis=1, keepdims=True) + EPSILON)
        value = (piece * scale * taper_ref[...]) * flags[:, w : w + 1]
        tapered[w, :rows, :] = value.astype(jnp.bfloat16)
    for pair in range(windows // 2):
        two = tapered[2 * pair : 2 * pair + 2].reshape(2 * LANES, WINDOW)
        value = lax.dot_general(
            table_ref[...], two, (((1,), (1,)), ((), ())), preferred_element_type=jnp.float32
        )
        value = value.reshape(groups, 2, GROUP, 2 * LANES)
        value = jnp.concatenate([value[..., :LANES], value[..., LANES:]], axis=2)
        out_ref[:, :, pair * 2 * GROUP : (pair + 1) * 2 * GROUP, :] = value.astype(jnp.bfloat16)


def cross_kernel(own_ref, other_ref, same_ref, cross_ref, table_ref, *rest, batch):
    out_ref, weights, wide, stacked = rest[-4:]
    count = same_ref.shape[0]
    rows = out_ref.shape[2]
    groups = own_ref.shape[0]
    depth = own_ref.shape[1]
    half = depth // 2
    bins = groups * GROUP
    for place, ref in enumerate((own_ref, other_ref)):
        base = place * depth
        weights[:, base : base + depth, :LANES] = ref[...]
        weights[:, base : base + half, LANES:] = ref[:, half:, :]
        weights[:, base + half : base + depth, LANES:] = -ref[:, :half, :]
    wide[0] = same_ref[...].astype(jnp.float32)
    wide[1] = cross_ref[...].astype(jnp.float32)
    lane = lax.broadcasted_iota(jnp.int32, (GROUP, depth), 1)
    sub = lax.broadcasted_iota(jnp.int32, (GROUP, depth), 0)
    mask = (lane % GROUP == sub).astype(jnp.float32)[None]

    def one_pair(pair, carry):
        parts = []
        for h in range(2):
            g = 2 * pair + h
            left = []
            for place in range(2):
                line = wide[place, :, pl.ds(g, 1), :]
                spread = jnp.broadcast_to(line, (count, GROUP, depth)) * mask
                left.append(spread.reshape(count * GROUP, depth).astype(jnp.bfloat16))
            value = jnp.dot(
                jnp.concatenate(left, axis=1), weights[g], preferred_element_type=jnp.float32
            )
            parts.append(value.reshape(count, GROUP, 2 * LANES))
        both = jnp.concatenate(parts, axis=1).astype(jnp.bfloat16)
        at = pl.multiple_of(pair * 2 * GROUP, 2 * GROUP)
        stacked[:, pl.ds(at, 2 * GROUP), :] = both[..., :LANES]
        stacked[:, pl.ds(bins + at, 2 * GROUP), :] = both[..., LANES:]
        return carry

    lax.fori_loop(0, groups // 2, one_pair, 0)
    padded = (rows + 15) // 16 * 16

    def one_batch(index, carry):
        turned = [stacked[index * batch + i].T[:padded] for i in range(batch)]
        value = jnp.dot(
            jnp.concatenate(turned, axis=0), table_ref[...], preferred_element_type=jnp.float32
        )
        for i in range(batch):
            part = value[i * padded : i * padded + rows]
            out_ref[0, index * batch + i] = part.astype(jnp.bfloat16)
        return carry

    lax.fori_loop(0, count // batch, one_batch, 0)


def whole(shape):
    return pl.BlockSpec(shape, lambda i: (0,) * len(shape))


def local(signal, valid_flags):
    rows = signal.shape[0]
    windows = signal.shape[1] // WINDOW
    chan, tm = lax.axis_size("chan"), lax.axis_size("tm")
    groups = WINDOW // 2 // GROUP
    depth = 2 * windows * GROUP
    half_rows = rows // tm
    own = pl.pallas_call(
        spectra_kernel,
        out_shape=jax.ShapeDtypeStruct((groups, 2, windows * GROUP, LANES), jnp.bfloat16),
        scratch_shapes=[pltpu.VMEM((windows, LANES, WINDOW), jnp.bfloat16)],
        compiler_params=pltpu.CompilerParams(vmem_limit_bytes=VMEM_LIMIT),
    )(signal, valid_flags, taper_table(WINDOW), forward_table(WINDOW))
    own = own.reshape(groups, depth, LANES)
    lines = jnp.transpose(own, (2, 0, 1))
    me = lax.axis_index("tm")
    same_half = lax.dynamic_slice_in_dim(lines, me * half_rows, half_rows, 0)
    other_half = lax.dynamic_slice_in_dim(lines, (1 - me) * half_rows, half_rows, 0)
    other = lax.ppermute(own, "tm", [(0, 1), (1, 0)])
    table = lag_table(WINDOW, LAGS, windows * tm)
    received = []
    for r in range(ROUNDS):
        pair = []
        for value, flip in ((same_half, 0), (other_half, 1)):
            moves = [
                (b * tm + t, ((b - r - 1) % chan) * tm + (t ^ flip))
                for b in range(chan)
                for t in range(tm)
            ]
            pair.append(lax.ppermute(value, ("chan", "tm"), moves))
        received.append(pair)
    out_shape = (ROUNDS, half_rows, rows, LAGS)
    batch = next(n for n in (4, 2, 1) if half_rows % n == 0)
    out = None
    for r in range(ROUNDS):
        args = [own, other, *received[r], table]
        specs = [whole(a.shape) for a in args]
        aliases = {}
        if out is not None:
            args.append(out)
            specs.append(pl.BlockSpec(memory_space=pl.ANY))
            aliases = {len(args) - 1: 0}
        out = pl.pallas_call(
            functools.partial(cross_kernel, batch=batch),
            grid=(1,),
            in_specs=specs,
            out_specs=pl.BlockSpec((1, half_rows, rows, LAGS), lambda i, r=r: (r, 0, 0, 0)),
            out_shape=jax.ShapeDtypeStruct(out_shape, jnp.bfloat16),
            scratch_shapes=[
                pltpu.VMEM((groups, tm * depth, 2 * LANES), jnp.bfloat16),
                pltpu.VMEM((tm, half_rows, groups, depth), jnp.float32),
                pltpu.VMEM((half_rows, WINDOW, LANES), jnp.bfloat16),
            ],
            input_output_aliases=aliases,
            compiler_params=pltpu.CompilerParams(vmem_limit_bytes=VMEM_LIMIT),
            cost_estimate=pl.CostEstimate(
                flops=2 * half_rows * rows * WINDOW * LAGS * 2, bytes_accessed=10**7, transcendentals=0
            ),
        )(*args)
    return out


def solution(mesh):
    return jax.shard_map(
        local,
        mesh=mesh,
        in_specs=(P(("group", "chan"), "tm"), P(("group", "chan"), "tm")),
        out_specs=P(None, "tm", ("group", "chan"), None),
        check_vma=False,
    )
```

profile of v0, /device:TPU:0, one launch (start us, length us, event | category | flops | bytes accessed | tf_op | source)
XLA Modules:
  0.0 122.2 jit_solution(11248865569778771409)
XLA Ops:
  0.0 1.4 %copy.13.flags_ref = s32[104,8]{1,0:T(8,128)} copy(s32[104,8]{0,1:T(8,128)} %param.6) | data formatting | bytes 6656 | tf_op args[1]
  1.4 6.8 %shard_map.55 = bf16[64,2,64,128]{3,2,1,0:T(8,128)(2,1)} custom-call(f32[104,8192]{1,0:T(8,128)} %signal_ref.1, s32[104,8]{1,0:T(8,128)} %copy.13.flags_ref, f32[1,1024]{1,0:T(1,128)} %constant.18.clone.taper_ref, bf16[1024,1024]{1,0:T(8,128)(2,1)} %constant.19.clone.table_ref), custom_call_target="tpu_custom_call" | custom-call | tf_op jit(solution)/shard_map/pallas_call | solution.py:129
  8.2 0.5 collective-permute-start
  8.7 4.8 %constant_dynamic-slice_fusion = (bf16[64,128,52]{2,1,0:T(8,128)(2,1)S(1)}, bf16[64,128,52]{2,1,0:T(8,128)(2,1)}) fusion(bf16[64,128,128]{2,1,0:T(8,128)(2,1)} %bitcast.4, s32[]{:T(128)S(6)} %select_n.7, s32[]{:T(128)S(6)} %select_n.6), kind=kLoop, calls=%fused_computation | loop fusion | bytes 3407880 | tf_op jit(solution)/shard_map/dynamic-slice.1
  13.5 2.7 %copy.16 = bf16[64,128,52]{1,0,2:T(8,128)(2,1)S(1)} copy(bf16[64,128,52]{2,1,0:T(8,128)(2,1)} %get-tuple-element.6) | data formatting | bytes 1703936
  16.2 5.6 %collective-permute-start.3 = (bf16[52,64,128]{2,1,0:T(8,128)(2,1)S(1)}, bf16[52,64,128]{2,1,0:T(8,128)(2,1)}, u32[]{:S(2)}, u32[]{:S(2)}) collective-permute-start(bf16[52,64,128]{2,1,0:T(8,128)(2,1)S(1)} %bitcast.7), channel_id=1, source_target_pairs={{0,14},{1,15},{2,0},{3,1},{4,2},{5,3},{6,4},{7,5},{8,6},{9,7},{10,... | collective-permute-start | bytes 2555912 | tf_op jit(solution)/shard_map/ppermute | solution.py:151
  21.8 2.4 %copy.17 = bf16[64,128,52]{1,0,2:T(8,128)(2,1)} copy(bf16[64,128,52]{2,1,0:T(8,128)(2,1)S(1)} %get-tuple-element.5) | data formatting | bytes 1703936
  24.2 0.3 collective-permute-start.4
  24.5 0.4 collective-permute-start.1
  25.0 0.1 collective-permute-start.2
  25.1 16.1 %collective-permute-done.3.same_ref = bf16[52,64,128]{2,1,0:T(8,128)(2,1)} collective-permute-done((bf16[52,64,128]{2,1,0:T(8,128)(2,1)S(1)}, bf16[52,64,128]{2,1,0:T(8,128)(2,1)}, u32[]{:S(2)}, u32[]{:S(2)}) %collective-permute-start.3) | collective-permute-done | bytes 852000 | tf_op jit(solution)/shard_map/ppermute | solution.py:151
  41.1 18.4 %collective-permute-done.4.cross_ref = bf16[52,64,128]{2,1,0:T(8,128)(2,1)S(1)} collective-permute-done((bf16[52,64,128]{2,1,0:T(8,128)(2,1)}, bf16[52,64,128]{2,1,0:T(8,128)(2,1)S(1)}, u32[]{:S(2)}, u32[]{:S(2)}) %collective-permute-start.4) | collective-permute-done | bytes 852000 | tf_op jit(solution)/shard_map/ppermute | solution.py:151
  59.5 0.0 copy-start.2
  59.5 0.0 collective-permute-done.other_ref
  59.5 0.9 copy-done.2
  60.4 25.7 %shard_map.56.rest_0_ = bf16[2,52,104,512]{3,2,1,0:T(8,128)(2,1)} custom-call(bf16[64,128,128]{2,1,0:T(8,128)(2,1)} %bitcast.5, bf16[64,128,128]{2,1,0:T(8,128)(2,1)} %collective-permute-done.other_ref, bf16[52,64,128]{2,1,0:T(8,128)(2,1)} %collective-permute-done.3.same_ref, bf16[52,64,128]{2,1,0:T(8,128)(2,1)} %copy-done.2, ...), custom_call_target="tpu_custom_call" | custom-call | flops 11341398016 | bytes 10000000 | tf_op jit(solution)/shard_map/pallas_call | solution.py:164
  86.1 0.0 collective-permute-done.1.same_ref
  86.1 0.0 copy-start
  86.1 9.5 %collective-permute-done.2.cross_ref = bf16[52,64,128]{2,1,0:T(8,128)(2,1)S(1)} collective-permute-done((bf16[52,64,128]{2,1,0:T(8,128)(2,1)}, bf16[52,64,128]{2,1,0:T(8,128)(2,1)S(1)}, u32[]{:S(2)}, u32[]{:S(2)}) %collective-permute-start.2) | collective-permute-done | bytes 852000 | tf_op jit(solution)/shard_map/ppermute | solution.py:151
  95.6 0.0 copy-done
  95.6 0.0 copy-start.1
  95.6 0.9 copy-done.1
  96.5 25.7 %shard_map.57 = bf16[2,52,104,512]{3,2,1,0:T(8,128)(2,1)} custom-call(bf16[64,128,128]{2,1,0:T(8,128)(2,1)} %bitcast.6, bf16[64,128,128]{2,1,0:T(8,128)(2,1)} %collective-permute-done.other_ref, bf16[52,64,128]{2,1,0:T(8,128)(2,1)} %copy-done, bf16[52,64,128]{2,1,0:T(8,128)(2,1)} %copy-done.1, ...), custom_call_target="tpu_custom_call", output_to_operand_aliasing={{}: (5, {})} | custom-call | flops 11341398016 | bytes 10000000 | tf_op jit(solution)/shard_map/pallas_call | solution.py:164
Async XLA Ops:
  8.2 51.2 %collective-permute-start = (bf16[64,128,128]{2,1,0:T(8,128)(2,1)}, bf16[64,128,128]{2,1,0:T(8,128)(2,1)}, u32[]{:S(2)}, u32[]{:S(2)}) collective-permute-start(bf16[64,128,128]{2,1,0:T(8,128)(2,1)} %bitcast.3), channel_id=1, source_target_pairs={{0,1},{1,0},{2,3},{3,2},{4,5},{5,4},{6,7},{7,6},{8,9},{9,8},{10,11... | collective-permute-start | bytes 6291464 | tf_op jit(solution)/shard_map/ppermute | solution.py:140
  16.2 24.9 %collective-permute-start.3 = (bf16[52,64,128]{2,1,0:T(8,128)(2,1)S(1)}, bf16[52,64,128]{2,1,0:T(8,128)(2,1)}, u32[]{:S(2)}, u32[]{:S(2)}) collective-permute-start(bf16[52,64,128]{2,1,0:T(8,128)(2,1)S(1)} %bitcast.7), channel_id=1, source_target_pairs={{0,14},{1,15},{2,0},{3,1},{4,2},{5,3},{6,4},{7,5},{8,6},{9,7},{10,... | collective-permute-start | bytes 2555912 | tf_op jit(solution)/shard_map/ppermute | solution.py:151
  24.2 35.3 %collective-permute-start.4 = (bf16[52,64,128]{2,1,0:T(8,128)(2,1)}, bf16[52,64,128]{2,1,0:T(8,128)(2,1)S(1)}, u32[]{:S(2)}, u32[]{:S(2)}) collective-permute-start(bf16[52,64,128]{2,1,0:T(8,128)(2,1)} %bitcast.9), channel_id=1, source_target_pairs={{0,15},{1,14},{2,1},{3,0},{4,3},{5,2},{6,5},{7,4},{8,7},{9,6},{10,... | collective-permute-start | bytes 2555912 | tf_op jit(solution)/shard_map/ppermute | solution.py:151
  24.5 61.5 %collective-permute-start.1 = (bf16[52,64,128]{2,1,0:T(8,128)(2,1)S(1)}, bf16[52,64,128]{2,1,0:T(8,128)(2,1)S(1)}, u32[]{:S(2)}, u32[]{:S(2)}) collective-permute-start(bf16[52,64,128]{2,1,0:T(8,128)(2,1)S(1)} %bitcast.8), channel_id=1, source_target_pairs={{0,12},{1,13},{2,14},{3,15},{4,0},{5,1},{6,2},{7,3},{8,4},{9,5},{1... | collective-permute-start | bytes 2555912 | tf_op jit(solution)/shard_map/ppermute | solution.py:151
  25.0 70.6 %collective-permute-start.2 = (bf16[52,64,128]{2,1,0:T(8,128)(2,1)}, bf16[52,64,128]{2,1,0:T(8,128)(2,1)S(1)}, u32[]{:S(2)}, u32[]{:S(2)}) collective-permute-start(bf16[52,64,128]{2,1,0:T(8,128)(2,1)} %bitcast.10), channel_id=1, source_target_pairs={{0,13},{1,12},{2,15},{3,14},{4,1},{5,0},{6,3},{7,2},{8,5},{9,4},{1... | collective-permute-start | bytes 2555912 | tf_op jit(solution)/shard_map/ppermute | solution.py:151
  59.5 0.9 copy-start.2
  86.1 9.5 %copy-start = (bf16[52,64,128]{2,1,0:T(8,128)(2,1)}, bf16[52,64,128]{2,1,0:T(8,128)(2,1)S(1)}, u32[]{:S(2)}) copy-start(bf16[52,64,128]{2,1,0:T(8,128)(2,1)S(1)} %collective-permute-done.1.same_ref) | copy-start | bytes 2555908
  95.6 0.9 copy-start.1
where the time goes:
time: 122 us
  Pallas kernels  58.2 us (48%)
  waiting for transfers between devices  43.9 us (36%)
  local copies, waits for them, and re-layouts  13.2 us (11%)
  starting transfers between devices  6.91 us (6%)
    pallas_call x2, Pallas kernels, local(): pl.pallas_call(functools.partial(cross_kernel, batch=batch), grid=(1,), i...  51.3 us
    ppermute x4, waiting for transfers between devices, local(): pair.append(lax.ppermute(value, ('chan', 'tm'), moves))  43.9 us
    unnamed x9, local copies, waits for them, and re-layouts  8.36 us
    pallas_call x1, Pallas kernels, local(): pl.pallas_call(spectra_kernel, out_shape=jax.ShapeDtypeStruct((groups, 2,...  6.83 us
    ppermute x4, starting transfers between devices, local(): pair.append(lax.ppermute(value, ('chan', 'tm'), moves))  6.46 us
    another operation x1, local copies, waits for them, and re-layouts  4.79 us
  transfers between devices with their start and end apart: 5, of which 3 were waited for; matrix products, arithmetic and copies ran while one was open for 8% of the time, Pallas kernels for 21%

commit v1 on v0

v1 whole, which is shorter than its diff:
```python
import functools

import jax
import jax.numpy as jnp
import numpy as np
from jax import lax
from jax.experimental import pallas as pl
from jax.experimental.pallas import tpu as pltpu
from jax.sharding import PartitionSpec as P

WINDOW = 1024
LAGS = 512
ROUNDS = 2
EPSILON = 1e-06
GROUP = 8
LANES = 128
VMEM_LIMIT = 56 * 1024 * 1024
CROSS_LIMIT = 40 * 1024 * 1024


def taper_table(window):
    t = np.arange(window, dtype=np.float32)
    return (0.5 - 0.5 * np.cos(2.0 * np.pi * t / window)).astype(np.float32)[None, :]


def forward_table(window):
    bins = window // 2
    f = np.arange(bins, dtype=np.int64)[:, None]
    t = np.arange(window, dtype=np.int64)[None, :]
    phases = 2.0 * np.pi / window * (f * t % window)
    table = np.stack([np.cos(phases), -np.sin(phases)])
    table = table.reshape(2, bins // GROUP, GROUP, window).transpose(1, 0, 2, 3)
    return table.reshape(window, window).astype(jnp.bfloat16)


def lag_table(window, lag_count, windows):
    f = np.arange(window // 2, dtype=np.int64)[:, None]
    tau = np.arange(lag_count, dtype=np.int64)[None, :] - lag_count // 2
    phases = 2.0 * np.pi / window * (f * tau % window)
    weight = np.where(f == 0, 1.0, 2.0) / (window * float(window * windows) ** 0.5)
    return np.concatenate([weight * np.cos(phases), -weight * np.sin(phases)]).astype(jnp.bfloat16)


def spectra_kernel(signal_ref, flags_ref, taper_ref, table_ref, out_ref, *rest):
    send_refs, (tapered, lines) = rest[:-2], rest[-2:]
    rows = signal_ref.shape[0]
    windows = flags_ref.shape[0]
    groups, depth = out_ref.shape[:2]
    half = depth // 2
    flags = flags_ref[...].astype(jnp.float32).T
    tapered[:, rows:, :] = jnp.zeros((windows, LANES - rows, WINDOW), jnp.bfloat16)
    for w in range(windows):
        piece = signal_ref[:, w * WINDOW : (w + 1) * WINDOW]
        scale = lax.rsqrt(jnp.mean(piece * piece, axis=1, keepdims=True) + EPSILON)
        value = (piece * scale * taper_ref[...]) * flags[:, w : w + 1]
        tapered[w, :rows, :] = value.astype(jnp.bfloat16)
    for pair in range(windows // 2):
        two = tapered[2 * pair : 2 * pair + 2].reshape(2 * LANES, WINDOW)
        value = lax.dot_general(
            table_ref[...], two, (((1,), (1,)), ((), ())), preferred_element_type=jnp.float32
        )
        value = value.reshape(groups, 2, GROUP, 2 * LANES)
        value = jnp.concatenate([value[..., :LANES], value[..., LANES:]], axis=2)
        value = value.astype(jnp.bfloat16)
        at = pair * 2 * GROUP
        out_ref[:, at : at + 2 * GROUP, :] = value[:, 0]
        out_ref[:, half + at : half + at + 2 * GROUP, :] = value[:, 1]

    def one_group(g, carry):
        lines[pl.ds(g, LANES, stride=groups), :] = out_ref[g].T.astype(jnp.float32)
        return carry

    lax.fori_loop(0, groups, one_group, 0, unroll=4)
    me = lax.axis_index("tm")
    count = send_refs[0].shape[0]
    for index, ref in enumerate(send_refs):
        chunk, flip = index // 2, index % 2
        start = (me if flip == 0 else 1 - me) * (rows // 2) + chunk * count
        start = pl.multiple_of(start * groups, groups)
        value = lines[pl.ds(start, count * groups), :]
        ref[...] = value.astype(jnp.bfloat16).reshape(count, groups, depth)


def cross_kernel(own_ref, other_ref, same_ref, cross_ref, table_ref, *rest, batch):
    out_ref, wide, stacked = rest[-3:]
    count = same_ref.shape[0]
    rows = out_ref.shape[2]
    groups, depth = own_ref.shape[:2]
    half = depth // 2
    bins = groups * GROUP
    wide[0] = same_ref[...].astype(jnp.float32)
    wide[1] = cross_ref[...].astype(jnp.float32)
    lane = lax.broadcasted_iota(jnp.int32, (GROUP, depth), 1)
    sub = lax.broadcasted_iota(jnp.int32, (GROUP, depth), 0)
    mask = (lane % GROUP == sub).astype(jnp.float32)[None]

    def one_pair(pair, carry):
        parts = []
        for h in range(2):
            g = 2 * pair + h
            left, real, imag = [], [], []
            for place, ref in enumerate((own_ref, other_ref)):
                line = wide[place, :, pl.ds(g, 1), :]
                spread = jnp.broadcast_to(line, (count, GROUP, depth)) * mask
                left.append(spread.reshape(count * GROUP, depth).astype(jnp.bfloat16))
                block = ref[g]
                real.append(block)
                imag += [block[half:], -block[:half]]
            weights = jnp.concatenate(
                [jnp.concatenate(real, axis=0), jnp.concatenate(imag, axis=0)], axis=1
            )
            value = jnp.dot(
                jnp.concatenate(left, axis=1), weights, preferred_element_type=jnp.float32
            )
            parts.append(value.reshape(count, GROUP, 2 * LANES))
        both = jnp.concatenate(parts, axis=1).astype(jnp.bfloat16)
        at = pl.multiple_of(pair * 2 * GROUP, 2 * GROUP)
        stacked[:, pl.ds(at, 2 * GROUP), :] = both[..., :LANES]
        stacked[:, pl.ds(bins + at, 2 * GROUP), :] = both[..., LANES:]
        return carry

    lax.fori_loop(0, groups // 2, one_pair, 0, unroll=2)
    padded = (rows + 15) // 16 * 16

    def one_batch(index, carry):
        turned = [stacked[index * batch + i].T[:padded] for i in range(batch)]
        value = jnp.dot(
            jnp.concatenate(turned, axis=0), table_ref[...], preferred_element_type=jnp.float32
        )
        for i in range(batch):
            part = value[i * padded : i * padded + rows]
            out_ref[0, index * batch + i] = part.astype(jnp.bfloat16)
        return carry

    lax.fori_loop(0, count // batch, one_batch, 0)


def whole(shape):
    return pl.BlockSpec(shape, lambda i: (0,) * len(shape))


def local(signal, valid_flags):
    rows = signal.shape[0]
    windows = signal.shape[1] // WINDOW
    chan, tm = lax.axis_size("chan"), lax.axis_size("tm")
    groups = WINDOW // 2 // GROUP
    depth = 2 * windows * GROUP
    half_rows = rows // tm
    chunks = 2 if half_rows % 2 == 0 else 1
    count = half_rows // chunks
    piece = jax.ShapeDtypeStruct((count, groups, depth), jnp.bfloat16)
    own, *sends = pl.pallas_call(
        spectra_kernel,
        out_shape=[jax.ShapeDtypeStruct((groups, depth, LANES), jnp.bfloat16)]
        + [piece] * (2 * chunks),
        scratch_shapes=[
            pltpu.VMEM((windows, LANES, WINDOW), jnp.bfloat16),
            pltpu.VMEM((LANES * groups, depth), jnp.float32),
        ],
        compiler_params=pltpu.CompilerParams(vmem_limit_bytes=VMEM_LIMIT),
    )(signal, valid_flags.T, taper_table(WINDOW), forward_table(WINDOW))
    table = lag_table(WINDOW, LAGS, windows * tm)

    def moved(value, steps, flip):
        moves = [
            (b * tm + t, ((b - steps) % chan) * tm + (t ^ flip))
            for b in range(chan)
            for t in range(tm)
        ]
        return lax.ppermute(value, ("chan", "tm"), moves)

    def chosen(q, flip, handed):
        if chan % 2:
            return sends[2 * q + flip]
        return jnp.where(lax.axis_index("chan") % 2 == 1, sends[2 * q + flip], handed)

    def paired(value, flip):
        if chan % 2:
            return moved(value, 1, flip)
        moves = [
            (b * tm + t, (b ^ 1) * tm + (t ^ (flip if b % 2 else 0)))
            for b in range(chan)
            for t in range(tm)
        ]
        return lax.ppermute(value, ("chan", "tm"), moves)

    received = {}
    other = None
    for q in range(chunks):
        for flip in range(2):
            received[1, q, flip] = moved(sends[2 * q + flip], 2, flip)
        if other is None:
            other = lax.ppermute(own, "tm", [(0, 1), (1, 0)])
    out_shape = (ROUNDS, half_rows, rows, LAGS)
    batch = next(n for n in (13, 8, 7, 5, 4, 3, 2, 1) if count % n == 0)

    def cross(out, r, q):
        args = [own, other, received[r, q, 0], received[r, q, 1], table]
        specs = [whole(a.shape) for a in args]
        aliases = {}
        if out is not None:
            args.append(out)
            specs.append(pl.BlockSpec(memory_space=pl.ANY))
            aliases = {len(args) - 1: 0}
        return pl.pallas_call(
            functools.partial(cross_kernel, batch=batch),
            grid=(1,),
            in_specs=specs,
            out_specs=pl.BlockSpec((1, count, rows, LAGS), lambda i, r=r, q=q: (r, q, 0, 0)),
            out_shape=jax.ShapeDtypeStruct(out_shape, jnp.bfloat16),
            scratch_shapes=[
                pltpu.VMEM((tm, count, groups, depth), jnp.float32),
                pltpu.VMEM((count, WINDOW, LANES), jnp.bfloat16),
            ],
            input_output_aliases=aliases,
            compiler_params=pltpu.CompilerParams(vmem_limit_bytes=CROSS_LIMIT),
            cost_estimate=pl.CostEstimate(
                flops=10**10, bytes_accessed=10**7, transcendentals=0
            ),
        )(*args)

    for flip in range(2):
        received[0, 0, flip] = paired(chosen(0, flip, received[1, 0, flip]), flip)
    out = cross(None, 1, 0)
    for q in range(1, chunks):
        came = [received[1, q, flip] for flip in range(2)]
        out, *came = lax.optimization_barrier((out, *came))
        values = [chosen(q, flip, came[flip]) for flip in range(2)]
        out, *values = lax.optimization_barrier((out, *values))
        for flip in range(2):
            received[0, q, flip] = paired(values[flip], flip)
        out = cross(out, 1, q)
        out = cross(out, 0, q - 1)
    return cross(out, 0, chunks - 1)


def solution(mesh):
    return jax.shard_map(
        local,
        mesh=mesh,
        in_specs=(P(("group", "chan"), "tm"), P(("group", "chan"), "tm")),
        out_specs=P(None, "tm", ("group", "chan"), None),
        check_vma=False,
    )
```

time: 122 us -> 90.7 us (0.74)
  waiting for transfers between devices: 43.9 us -> 17 us
  local copies, waits for them, and re-layouts: 13.2 us -> 2.82 us
  starting transfers between devices: 6.91 us -> 13.1 us
    ppermute x4 -> x8, waiting for transfers between devices: 43.9 us -> 17 us  [the longest x4 17 us: moved(): return lax.ppermute(value, ('chan', 'tm'), moves)]
    ppermute x4 -> x8, starting transfers between devices: 6.46 us -> 12.7 us  [the longest x4 7.33 us: paired(): return lax.ppermute(value, ('chan', 'tm'), moves)]
    unnamed x9 -> x8, local copies, waits for them, and re-layouts: 8.36 us -> 2.82 us
    another operation x1 -> x0, local copies, waits for them, and re-layouts: 4.79 us -> none
    pallas_call x3 -> x5, Pallas kernels: 58.2 us -> 57.1 us  [the longest x4 46 us: cross(): pl.pallas_call(functools.partial(cross_kernel, batch=batch), grid=(1,), i...]
  transfers between devices with their start and end apart: 5 -> 9, of which waited for: 3 -> 3; matrix products, arithmetic and copies ran while one was open for 8% -> 0% of each run, Pallas kernels for 21% -> 38%
where the time goes in v1:
time: 90.7 us; the launch traced here: 90.3 us
  Pallas kernels  57.1 us (63%)
  waiting for transfers between devices  17 us (19%)
  starting transfers between devices  13.1 us (14%)
  local copies, waits for them, and re-layouts  2.82 us (3%)
    pallas_call x4, Pallas kernels, cross(): pl.pallas_call(functools.partial(cross_kernel, batch=batch), grid=(1,), i...  46 us
    ppermute x4, waiting for transfers between devices, moved(): return lax.ppermute(value, ('chan', 'tm'), moves)  17 us
    pallas_call x1, Pallas kernels, local(): pl.pallas_call(spectra_kernel, out_shape=[jax.ShapeDtypeStruct((groups, d...  11.1 us
    ppermute x4, starting transfers between devices, paired(): return lax.ppermute(value, ('chan', 'tm'), moves)  7.33 us
    ppermute x4, starting transfers between devices, moved(): return lax.ppermute(value, ('chan', 'tm'), moves)  5.33 us
    unnamed x8, local copies, waits for them, and re-layouts  2.82 us
  transfers between devices with their start and end apart: 9, of which 3 were waited for; matrix products, arithmetic and copies ran while one was open for 0% of the time, Pallas kernels for 38%

profile of v1, /device:TPU:0, one launch (start us, length us, event | category | flops | bytes accessed | tf_op | source)
XLA Modules:
  0.0 90.3 jit_solution(15796530173047786212)
XLA Ops:
  0.0 11.1 %shard_map.55 = (bf16[64,128,128]{2,1,0:T(8,128)(2,1)}, bf16[26,64,128]{2,1,0:T(8,128)(2,1)}, bf16[26,64,128]{2,1,0:T(8,128)(2,1)}, bf16[26,64,128]{2,1,0:T(8,128)(2,1)}, bf16[26,64,128]{2,1,0:T(8,128)(2,1)}) custom-call(f32[104,8192]{1,0:T(8,128)} %signal_ref.1, s32[8,104]{1,0:T(8,128)} %bitcast.1, f32[1,1024]{1,0:T(1,128)} %constant.32.clone.taper_ref, ...), custom_call_target="tpu_custom_call" | custom-call | tf_op jit(solution)/shard_map/pallas_call | solution.py:152
  11.1 0.5 collective-permute-start
  11.6 4.6 %collective-permute-start.1 = (bf16[26,64,128]{2,1,0:T(8,128)(2,1)}, bf16[26,64,128]{2,1,0:T(8,128)(2,1)S(1)}, u32[]{:S(2)}, u32[]{:S(2)}) collective-permute-start(bf16[26,64,128]{2,1,0:T(8,128)(2,1)} %get-tuple-element.17), channel_id=1, source_target_pairs={{0,12},{1,13},{2,14},{3,15},{4,0},{5,1},{6,2},{7,3},{8,4},{9,5},{1... | collective-permute-start | bytes 1277960 | tf_op jit(solution)/shard_map/ppermute | solution.py:170
  16.2 0.3 collective-permute-start.2
  16.4 0.5 collective-permute-start.3
  16.9 9.7 %collective-permute-done.1.same_ref = bf16[26,64,128]{2,1,0:T(8,128)(2,1)S(1)} collective-permute-done((bf16[26,64,128]{2,1,0:T(8,128)(2,1)}, bf16[26,64,128]{2,1,0:T(8,128)(2,1)S(1)}, u32[]{:S(2)}, u32[]{:S(2)}) %collective-permute-start.1) | collective-permute-done | bytes 426016 | tf_op jit(solution)/shard_map/ppermute | solution.py:170
  26.7 2.6 %collective-permute-start.7 = (bf16[26,64,128]{2,1,0:T(8,128)(2,1)S(1)}, bf16[26,64,128]{2,1,0:T(8,128)(2,1)S(1)}, u32[]{:S(2)}, u32[]{:S(2)}) collective-permute-start(bf16[26,64,128]{2,1,0:T(8,128)(2,1)S(1)} %broadcast_select_fusion.1), channel_id=1, source_target_pairs={{0,2},{1,3},{2,0},{3,1},{4,6},{5,7},{6,4},{7,5},{8,10},{9,11},{10,... | collective-permute-start | bytes 1277960 | tf_op jit(solution)/shard_map/ppermute | solution.py:185
  29.3 6.5 %collective-permute-done.2.cross_ref = bf16[26,64,128]{2,1,0:T(8,128)(2,1)S(1)} collective-permute-done((bf16[26,64,128]{2,1,0:T(8,128)(2,1)}, bf16[26,64,128]{2,1,0:T(8,128)(2,1)S(1)}, u32[]{:S(2)}, u32[]{:S(2)}) %collective-permute-start.2) | collective-permute-done | bytes 426016 | tf_op jit(solution)/shard_map/ppermute | solution.py:170
  35.8 2.7 %collective-permute-start.8 = (bf16[26,64,128]{2,1,0:T(8,128)(2,1)S(1)}, bf16[26,64,128]{2,1,0:T(8,128)(2,1)S(1)}, u32[]{:S(2)}, u32[]{:S(2)}) collective-permute-start(bf16[26,64,128]{2,1,0:T(8,128)(2,1)S(1)} %broadcast_select_fusion), channel_id=1, source_target_pairs={{0,2},{1,3},{2,1},{3,0},{4,6},{5,7},{6,5},{7,4},{8,10},{9,11},{10,... | collective-permute-start | bytes 1277960 | tf_op jit(solution)/shard_map/ppermute | solution.py:185
  38.5 0.0 collective-permute-done.other_ref
  38.5 1.6 %copy-done = bf16[64,128,128]{2,1,0:T(8,128)(2,1)S(1)} copy-done((bf16[64,128,128]{2,1,0:T(8,128)(2,1)S(1)}, bf16[64,128,128]{2,1,0:T(8,128)(2,1)}, u32[]{:S(2)}) %copy-start) | copy-done | bytes 2097176
  40.0 1.2 %copy-done.1 = bf16[1024,512]{1,0:T(8,128)(2,1)S(1)} copy-done((bf16[1024,512]{1,0:T(8,128)(2,1)S(1)}, bf16[1024,512]{1,0:T(8,128)(2,1)}, u32[]{:S(2)}) %copy-start.1) | copy-done | bytes 1048600
  41.3 11.5 %shard_map.56.rest_0_ = bf16[2,52,104,512]{3,2,1,0:T(8,128)(2,1)} custom-call(bf16[64,128,128]{2,1,0:T(8,128)(2,1)S(1)} %copy-done, bf16[64,128,128]{2,1,0:T(8,128)(2,1)} %collective-permute-done.other_ref, bf16[26,64,128]{2,1,0:T(8,128)(2,1)S(1)} %collective-permute-done.1.same_ref, bf16[26,64,128]{2,1,0:T(8,128)(2,1)S(1)} %collective-permute-done.2.cross_ref, ...), custom_call_target="tpu_custom_call" | custom-call | flops 10000000000 | bytes 10000000 | tf_op jit(solution)/shard_map/pallas_call | solution.py:205
  52.8 0.0 collective-permute-done.3.same_ref
  52.8 0.8 collective-permute-done.4.cross_ref
  53.6 0.1 broadcast_select_fusion.2
  53.7 1.6 %collective-permute-start.5 = (bf16[26,64,128]{2,1,0:T(8,128)(2,1)S(1)}, bf16[26,64,128]{2,1,0:T(8,128)(2,1)S(1)}, u32[]{:S(2)}, u32[]{:S(2)}) collective-permute-start(bf16[26,64,128]{2,1,0:T(8,128)(2,1)S(1)} %get-tuple-element.24), channel_id=1, source_target_pairs={{0,2},{1,3},{2,0},{3,1},{4,6},{5,7},{6,4},{7,5},{8,10},{9,11},{10,... | collective-permute-start | bytes 1277960 | tf_op jit(solution)/shard_map/ppermute | solution.py:185
  55.3 0.5 collective-permute-start.6
  55.8 11.5 %shard_map.57.rest_0_ = bf16[2,52,104,512]{3,2,1,0:T(8,128)(2,1)} custom-call(bf16[64,128,128]{2,1,0:T(8,128)(2,1)S(1)} %copy-done, bf16[64,128,128]{2,1,0:T(8,128)(2,1)} %collective-permute-done.other_ref, bf16[26,64,128]{2,1,0:T(8,128)(2,1)S(1)} %collective-permute-done.3.same_ref, ...), custom_call_target="tpu_custom_call", output_to_operand_aliasing={{}: (5, {})} | custom-call | flops 10000000000 | bytes 10000000 | tf_op jit(solution)/shard_map/pallas_call | solution.py:205
  67.3 0.0 collective-permute-done.7.same_ref
  67.3 0.0 collective-permute-done.8.cross_ref
  67.3 11.5 %shard_map.58.rest_0_ = bf16[2,52,104,512]{3,2,1,0:T(8,128)(2,1)} custom-call(bf16[64,128,128]{2,1,0:T(8,128)(2,1)S(1)} %copy-done, bf16[64,128,128]{2,1,0:T(8,128)(2,1)} %collective-permute-done.other_ref, bf16[26,64,128]{2,1,0:T(8,128)(2,1)S(1)} %collective-permute-done.7.same_ref, ...), custom_call_target="tpu_custom_call", output_to_operand_aliasing={{}: (5, {})} | custom-call | flops 10000000000 | bytes 10000000 | tf_op jit(solution)/shard_map/pallas_call | solution.py:205
  78.8 0.0 collective-permute-done.5.same_ref
  78.8 11.5 %shard_map.59 = bf16[2,52,104,512]{3,2,1,0:T(8,128)(2,1)} custom-call(bf16[64,128,128]{2,1,0:T(8,128)(2,1)S(1)} %copy-done, bf16[64,128,128]{2,1,0:T(8,128)(2,1)} %collective-permute-done.other_ref, bf16[26,64,128]{2,1,0:T(8,128)(2,1)S(1)} %collective-permute-done.5.same_ref, ...), custom_call_target="tpu_custom_call", output_to_operand_aliasing={{}: (5, {})} | custom-call | flops 10000000000 | bytes 10000000 | tf_op jit(solution)/shard_map/pallas_call | solution.py:205
  (10 shorter events, 0.1 us)
Async XLA Ops:
  11.1 27.3 %collective-permute-start = (bf16[64,128,128]{2,1,0:T(8,128)(2,1)}, bf16[64,128,128]{2,1,0:T(8,128)(2,1)}, u32[]{:S(2)}, u32[]{:S(2)}) collective-permute-start(bf16[64,128,128]{2,1,0:T(8,128)(2,1)} %get-tuple-element.16.own_ref), channel_id=1, source_target_pairs={{0,1},{1,0},{2,3},{3,2},{4,5},{5,4},{6,7},{7,6},{8,9},{9,8},{10,11... | collective-permute-start | bytes 6291464 | tf_op jit(solution)/shard_map/ppermute | solution.py:193
  11.6 15.0 %collective-permute-start.1 = (bf16[26,64,128]{2,1,0:T(8,128)(2,1)}, bf16[26,64,128]{2,1,0:T(8,128)(2,1)S(1)}, u32[]{:S(2)}, u32[]{:S(2)}) collective-permute-start(bf16[26,64,128]{2,1,0:T(8,128)(2,1)} %get-tuple-element.17), channel_id=1, source_target_pairs={{0,12},{1,13},{2,14},{3,15},{4,0},{5,1},{6,2},{7,3},{8,4},{9,5},{1... | collective-permute-start | bytes 1277960 | tf_op jit(solution)/shard_map/ppermute | solution.py:170
  16.2 19.6 %collective-permute-start.2 = (bf16[26,64,128]{2,1,0:T(8,128)(2,1)}, bf16[26,64,128]{2,1,0:T(8,128)(2,1)S(1)}, u32[]{:S(2)}, u32[]{:S(2)}) collective-permute-start(bf16[26,64,128]{2,1,0:T(8,128)(2,1)} %get-tuple-element.18), channel_id=1, source_target_pairs={{0,13},{1,12},{2,15},{3,14},{4,1},{5,0},{6,3},{7,2},{8,5},{9,4},{1... | collective-permute-start | bytes 1277960 | tf_op jit(solution)/shard_map/ppermute | solution.py:170
  16.4 36.3 %collective-permute-start.3 = (bf16[26,64,128]{2,1,0:T(8,128)(2,1)}, bf16[26,64,128]{2,1,0:T(8,128)(2,1)S(1)}, u32[]{:S(2)}, u32[]{:S(2)}) collective-permute-start(bf16[26,64,128]{2,1,0:T(8,128)(2,1)} %get-tuple-element.19), channel_id=1, source_target_pairs={{0,12},{1,13},{2,14},{3,15},{4,0},{5,1},{6,2},{7,3},{8,4},{9,5},{1... | collective-permute-start | bytes 1277960 | tf_op jit(solution)/shard_map/ppermute | solution.py:170
  16.9 36.7 %collective-permute-start.4 = (bf16[26,64,128]{2,1,0:T(8,128)(2,1)}, bf16[26,64,128]{2,1,0:T(8,128)(2,1)S(1)}, u32[]{:S(2)}, u32[]{:S(2)}) collective-permute-start(bf16[26,64,128]{2,1,0:T(8,128)(2,1)} %get-tuple-element.20), channel_id=1, source_target_pairs={{0,13},{1,12},{2,15},{3,14},{4,1},{5,0},{6,3},{7,2},{8,5},{9,4},{1... | collective-permute-start | bytes 1277960 | tf_op jit(solution)/shard_map/ppermute | solution.py:170
  26.7 40.6 %collective-permute-start.7 = (bf16[26,64,128]{2,1,0:T(8,128)(2,1)S(1)}, bf16[26,64,128]{2,1,0:T(8,128)(2,1)S(1)}, u32[]{:S(2)}, u32[]{:S(2)}) collective-permute-start(bf16[26,64,128]{2,1,0:T(8,128)(2,1)S(1)} %broadcast_select_fusion.1), channel_id=1, source_target_pairs={{0,2},{1,3},{2,0},{3,1},{4,6},{5,7},{6,4},{7,5},{8,10},{9,11},{10,... | collective-permute-start | bytes 1277960 | tf_op jit(solution)/shard_map/ppermute | solution.py:185
  35.7 17.9 %copy-start.2 = (bf16[26,64,128]{2,1,0:T(8,128)(2,1)S(1)}, bf16[26,64,128]{2,1,0:T(8,128)(2,1)}, u32[]{:S(2)}) copy-start(bf16[26,64,128]{2,1,0:T(8,128)(2,1)} %get-tuple-element.19) | copy-start | bytes 1277956
  35.7 17.9 %copy-start.3 = (bf16[26,64,128]{2,1,0:T(8,128)(2,1)S(1)}, bf16[26,64,128]{2,1,0:T(8,128)(2,1)}, u32[]{:S(2)}) copy-start(bf16[26,64,128]{2,1,0:T(8,128)(2,1)} %get-tuple-element.20) | copy-start | bytes 1277956
  35.8 31.5 %collective-permute-start.8 = (bf16[26,64,128]{2,1,0:T(8,128)(2,1)S(1)}, bf16[26,64,128]{2,1,0:T(8,128)(2,1)S(1)}, u32[]{:S(2)}, u32[]{:S(2)}) collective-permute-start(bf16[26,64,128]{2,1,0:T(8,128)(2,1)S(1)} %broadcast_select_fusion), channel_id=1, source_target_pairs={{0,2},{1,3},{2,1},{3,0},{4,6},{5,7},{6,5},{7,4},{8,10},{9,11},{10,... | collective-permute-start | bytes 1277960 | tf_op jit(solution)/shard_map/ppermute | solution.py:185
  38.5 1.6 %copy-start = (bf16[64,128,128]{2,1,0:T(8,128)(2,1)S(1)}, bf16[64,128,128]{2,1,0:T(8,128)(2,1)}, u32[]{:S(2)}) copy-start(bf16[64,128,128]{2,1,0:T(8,128)(2,1)} %get-tuple-element.16.own_ref) | copy-start | bytes 6291460
  40.0 1.2 %copy-start.1 = (bf16[1024,512]{1,0:T(8,128)(2,1)S(1)}, bf16[1024,512]{1,0:T(8,128)(2,1)}, u32[]{:S(2)}) copy-start(bf16[1024,512]{1,0:T(8,128)(2,1)} %constant.34.clone.table_ref) | copy-start | bytes 3145732
  53.7 25.1 %collective-permute-start.5 = (bf16[26,64,128]{2,1,0:T(8,128)(2,1)S(1)}, bf16[26,64,128]{2,1,0:T(8,128)(2,1)S(1)}, u32[]{:S(2)}, u32[]{:S(2)}) collective-permute-start(bf16[26,64,128]{2,1,0:T(8,128)(2,1)S(1)} %get-tuple-element.24), channel_id=1, source_target_pairs={{0,2},{1,3},{2,0},{3,1},{4,6},{5,7},{6,4},{7,5},{8,10},{9,11},{10,... | collective-permute-start | bytes 1277960 | tf_op jit(solution)/shard_map/ppermute | solution.py:185
  55.3 23.5 %collective-permute-start.6 = (bf16[26,64,128]{2,1,0:T(8,128)(2,1)S(1)}, bf16[26,64,128]{2,1,0:T(8,128)(2,1)S(1)}, u32[]{:S(2)}, u32[]{:S(2)}) collective-permute-start(bf16[26,64,128]{2,1,0:T(8,128)(2,1)S(1)} %get-tuple-element.25), channel_id=1, source_target_pairs={{0,2},{1,3},{2,1},{3,0},{4,6},{5,7},{6,5},{7,4},{8,10},{9,11},{10,... | collective-permute-start | bytes 1277960 | tf_op jit(solution)/shard_map/ppermute | solution.py:185

commit v2 on v1

--- a/solution.py
+++ b/solution.py
@@ -15,7 +15,7 @@
 GROUP = 8
 LANES = 128
 VMEM_LIMIT = 56 * 1024 * 1024
-CROSS_LIMIT = 40 * 1024 * 1024
+CROSS_LIMIT = 32 * 1024 * 1024
 
 
 def taper_table(window):
@@ -70,7 +70,7 @@
         lines[pl.ds(g, LANES, stride=groups), :] = out_ref[g].T.astype(jnp.float32)
         return carry
 
-    lax.fori_loop(0, groups, one_group, 0, unroll=4)
+    lax.fori_loop(0, groups, one_group, 0, unroll=16)
     me = lax.axis_index("tm")
     count = send_refs[0].shape[0]
     for index, ref in enumerate(send_refs):
@@ -119,7 +119,7 @@
         stacked[:, pl.ds(bins + at, 2 * GROUP), :] = both[..., LANES:]
         return carry
 
-    lax.fori_loop(0, groups // 2, one_pair, 0, unroll=2)
+    lax.fori_loop(0, groups // 2, one_pair, 0, unroll=8)
     padded = (rows + 15) // 16 * 16
 
     def one_batch(index, carry):
@@ -133,10 +133,6 @@
         return carry
 
     lax.fori_loop(0, count // batch, one_batch, 0)
-
-
-def whole(shape):
-    return pl.BlockSpec(shape, lambda i: (0,) * len(shape))
 
 
 def local(signal, valid_flags):
@@ -196,7 +192,7 @@
 
     def cross(out, r, q):
         args = [own, other, received[r, q, 0], received[r, q, 1], table]
-        specs = [whole(a.shape) for a in args]
+        specs = [pl.BlockSpec(memory_space=pltpu.VMEM) for _ in args]
         aliases = {}
         if out is not None:
             args.append(out)

time: 90.7 us -> 84.5 us (0.932)
  Pallas kernels: 57.1 us -> 49.1 us
  waiting for transfers between devices: 17 us -> 19 us
    pallas_call x4, Pallas kernels: 46 us -> 38.3 us  [cross(): pl.pallas_call(functools.partial(cross_kernel, batch=batch), grid=(1,), i...]
    ppermute x4, waiting for transfers between devices: 17 us -> 19 us  [moved(): return lax.ppermute(value, ('chan', 'tm'), moves)]
  transfers between devices with their start and end apart: 9 -> 9, of which waited for: 3 -> 3; matrix products, arithmetic and copies ran while one was open for 0% -> 0% of each run, Pallas kernels for 38% -> 34%
where the time goes in v2:
time: 84.5 us; the launch traced here: 84.2 us
  Pallas kernels  49.1 us (58%)
  waiting for transfers between devices  19 us (22%)
  starting transfers between devices  13.1 us (16%)
  local copies, waits for them, and re-layouts  2.82 us (3%)
    pallas_call x4, Pallas kernels, cross(): pl.pallas_call(functools.partial(cross_kernel, batch=batch), grid=(1,), i...  38.3 us
    ppermute x4, waiting for transfers between devices, moved(): return lax.ppermute(value, ('chan', 'tm'), moves)  19 us
    pallas_call x1, Pallas kernels, local(): pl.pallas_call(spectra_kernel, out_shape=[jax.ShapeDtypeStruct((groups, d...  10.8 us
    ppermute x4, starting transfers between devices, paired(): return lax.ppermute(value, ('chan', 'tm'), moves)  7.33 us
    ppermute x4, starting transfers between devices, moved(): return lax.ppermute(value, ('chan', 'tm'), moves)  5.33 us
    unnamed x8, local copies, waits for them, and re-layouts  2.82 us
  transfers between devices with their start and end apart: 9, of which 3 were waited for; matrix products, arithmetic and copies ran while one was open for 0% of the time, Pallas kernels for 34%

profile of v2, /device:TPU:0, one launch (start us, length us, event | category | flops | bytes accessed | tf_op | source)
XLA Modules:
  0.0 84.2 jit_solution(9619314923539325015)
XLA Ops:
  0.0 10.8 %shard_map.55 = (bf16[64,128,128]{2,1,0:T(8,128)(2,1)}, bf16[26,64,128]{2,1,0:T(8,128)(2,1)}, bf16[26,64,128]{2,1,0:T(8,128)(2,1)}, bf16[26,64,128]{2,1,0:T(8,128)(2,1)}, bf16[26,64,128]{2,1,0:T(8,128)(2,1)}) custom-call(f32[104,8192]{1,0:T(8,128)} %signal_ref.1, s32[8,104]{1,0:T(8,128)} %bitcast.1, f32[1,1024]{1,0:T(1,128)} %constant.32.clone.taper_ref, ...), custom_call_target="tpu_custom_call" | custom-call | tf_op jit(solution)/shard_map/pallas_call | solution.py:148
  10.8 0.5 collective-permute-start
  11.2 4.6 %collective-permute-start.1 = (bf16[26,64,128]{2,1,0:T(8,128)(2,1)}, bf16[26,64,128]{2,1,0:T(8,128)(2,1)S(1)}, u32[]{:S(2)}, u32[]{:S(2)}) collective-permute-start(bf16[26,64,128]{2,1,0:T(8,128)(2,1)} %get-tuple-element.17), channel_id=1, source_target_pairs={{0,12},{1,13},{2,14},{3,15},{4,0},{5,1},{6,2},{7,3},{8,4},{9,5},{1... | collective-permute-start | bytes 1277960 | tf_op jit(solution)/shard_map/ppermute | solution.py:166
  15.8 0.3 collective-permute-start.2
  16.1 0.4 collective-permute-start.3
  16.5 0.0 collective-permute-start.4
  16.5 9.7 %collective-permute-done.1.same_ref = bf16[26,64,128]{2,1,0:T(8,128)(2,1)S(1)} collective-permute-done((bf16[26,64,128]{2,1,0:T(8,128)(2,1)}, bf16[26,64,128]{2,1,0:T(8,128)(2,1)S(1)}, u32[]{:S(2)}, u32[]{:S(2)}) %collective-permute-start.1) | collective-permute-done | bytes 426016 | tf_op jit(solution)/shard_map/ppermute | solution.py:166
  26.3 2.6 %collective-permute-start.7 = (bf16[26,64,128]{2,1,0:T(8,128)(2,1)S(1)}, bf16[26,64,128]{2,1,0:T(8,128)(2,1)S(1)}, u32[]{:S(2)}, u32[]{:S(2)}) collective-permute-start(bf16[26,64,128]{2,1,0:T(8,128)(2,1)S(1)} %broadcast_select_fusion.1), channel_id=1, source_target_pairs={{0,2},{1,3},{2,0},{3,1},{4,6},{5,7},{6,4},{7,5},{8,10},{9,11},{10,... | collective-permute-start | bytes 1277960 | tf_op jit(solution)/shard_map/ppermute | solution.py:181
  28.9 6.5 %collective-permute-done.2.cross_ref = bf16[26,64,128]{2,1,0:T(8,128)(2,1)S(1)} collective-permute-done((bf16[26,64,128]{2,1,0:T(8,128)(2,1)}, bf16[26,64,128]{2,1,0:T(8,128)(2,1)S(1)}, u32[]{:S(2)}, u32[]{:S(2)}) %collective-permute-start.2) | collective-permute-done | bytes 426016 | tf_op jit(solution)/shard_map/ppermute | solution.py:166
  35.4 2.7 %collective-permute-start.8 = (bf16[26,64,128]{2,1,0:T(8,128)(2,1)S(1)}, bf16[26,64,128]{2,1,0:T(8,128)(2,1)S(1)}, u32[]{:S(2)}, u32[]{:S(2)}) collective-permute-start(bf16[26,64,128]{2,1,0:T(8,128)(2,1)S(1)} %broadcast_select_fusion), channel_id=1, source_target_pairs={{0,2},{1,3},{2,1},{3,0},{4,6},{5,7},{6,5},{7,4},{8,10},{9,11},{10,... | collective-permute-start | bytes 1277960 | tf_op jit(solution)/shard_map/ppermute | solution.py:181
  38.1 0.0 collective-permute-done.other_ref
  38.1 1.6 %copy-done = bf16[64,128,128]{2,1,0:T(8,128)(2,1)S(1)} copy-done((bf16[64,128,128]{2,1,0:T(8,128)(2,1)S(1)}, bf16[64,128,128]{2,1,0:T(8,128)(2,1)}, u32[]{:S(2)}) %copy-start) | copy-done | bytes 2097176
  39.7 1.2 %copy-done.1 = bf16[1024,512]{1,0:T(8,128)(2,1)S(1)} copy-done((bf16[1024,512]{1,0:T(8,128)(2,1)S(1)}, bf16[1024,512]{1,0:T(8,128)(2,1)}, u32[]{:S(2)}) %copy-start.1) | copy-done | bytes 1048600
  40.9 9.6 %shard_map.56.rest_0_ = bf16[2,52,104,512]{3,2,1,0:T(8,128)(2,1)} custom-call(bf16[64,128,128]{2,1,0:T(8,128)(2,1)S(1)} %copy-done, bf16[64,128,128]{2,1,0:T(8,128)(2,1)} %collective-permute-done.other_ref, bf16[26,64,128]{2,1,0:T(8,128)(2,1)S(1)} %collective-permute-done.1.same_ref, bf16[26,64,128]{2,1,0:T(8,128)(2,1)S(1)} %collective-permute-done.2.cross_ref, ...), custom_call_target="tpu_custom_call" | custom-call | flops 10000000000 | bytes 10000000 | tf_op jit(solution)/shard_map/pallas_call | solution.py:201
  50.5 0.0 collective-permute-done.3.same_ref
  50.5 2.8 %collective-permute-done.4.cross_ref = bf16[26,64,128]{2,1,0:T(8,128)(2,1)S(1)} collective-permute-done((bf16[26,64,128]{2,1,0:T(8,128)(2,1)}, bf16[26,64,128]{2,1,0:T(8,128)(2,1)S(1)}, u32[]{:S(2)}, u32[]{:S(2)}) %collective-permute-start.4) | collective-permute-done | bytes 426016 | tf_op jit(solution)/shard_map/ppermute | solution.py:166
  53.3 0.1 broadcast_select_fusion.2
  53.4 1.6 %collective-permute-start.5 = (bf16[26,64,128]{2,1,0:T(8,128)(2,1)S(1)}, bf16[26,64,128]{2,1,0:T(8,128)(2,1)S(1)}, u32[]{:S(2)}, u32[]{:S(2)}) collective-permute-start(bf16[26,64,128]{2,1,0:T(8,128)(2,1)S(1)} %get-tuple-element.24), channel_id=1, source_target_pairs={{0,2},{1,3},{2,0},{3,1},{4,6},{5,7},{6,4},{7,5},{8,10},{9,11},{10,... | collective-permute-start | bytes 1277960 | tf_op jit(solution)/shard_map/ppermute | solution.py:181
  54.9 0.5 collective-permute-start.6
  55.4 9.6 %shard_map.57.rest_0_ = bf16[2,52,104,512]{3,2,1,0:T(8,128)(2,1)} custom-call(bf16[64,128,128]{2,1,0:T(8,128)(2,1)S(1)} %copy-done, bf16[64,128,128]{2,1,0:T(8,128)(2,1)} %collective-permute-done.other_ref, bf16[26,64,128]{2,1,0:T(8,128)(2,1)S(1)} %collective-permute-done.3.same_ref, ...), custom_call_target="tpu_custom_call", output_to_operand_aliasing={{}: (5, {})} | custom-call | flops 10000000000 | bytes 10000000 | tf_op jit(solution)/shard_map/pallas_call | solution.py:201
  65.1 0.0 collective-permute-done.7.same_ref
  65.1 0.0 collective-permute-done.8.cross_ref
  65.1 9.6 %shard_map.58.rest_0_ = bf16[2,52,104,512]{3,2,1,0:T(8,128)(2,1)} custom-call(bf16[64,128,128]{2,1,0:T(8,128)(2,1)S(1)} %copy-done, bf16[64,128,128]{2,1,0:T(8,128)(2,1)} %collective-permute-done.other_ref, bf16[26,64,128]{2,1,0:T(8,128)(2,1)S(1)} %collective-permute-done.7.same_ref, ...), custom_call_target="tpu_custom_call", output_to_operand_aliasing={{}: (5, {})} | custom-call | flops 10000000000 | bytes 10000000 | tf_op jit(solution)/shard_map/pallas_call | solution.py:201
  74.6 9.6 %shard_map.59 = bf16[2,52,104,512]{3,2,1,0:T(8,128)(2,1)} custom-call(bf16[64,128,128]{2,1,0:T(8,128)(2,1)S(1)} %copy-done, bf16[64,128,128]{2,1,0:T(8,128)(2,1)} %collective-permute-done.other_ref, bf16[26,64,128]{2,1,0:T(8,128)(2,1)S(1)} %collective-permute-done.5.same_ref, ...), custom_call_target="tpu_custom_call", output_to_operand_aliasing={{}: (5, {})} | custom-call | flops 10000000000 | bytes 10000000 | tf_op jit(solution)/shard_map/pallas_call | solution.py:201
  (10 shorter events, 0.1 us)
Async XLA Ops:
  10.8 27.3 %collective-permute-start = (bf16[64,128,128]{2,1,0:T(8,128)(2,1)}, bf16[64,128,128]{2,1,0:T(8,128)(2,1)}, u32[]{:S(2)}, u32[]{:S(2)}) collective-permute-start(bf16[64,128,128]{2,1,0:T(8,128)(2,1)} %get-tuple-element.16.own_ref), channel_id=1, source_target_pairs={{0,1},{1,0},{2,3},{3,2},{4,5},{5,4},{6,7},{7,6},{8,9},{9,8},{10,11... | collective-permute-start | bytes 6291464 | tf_op jit(solution)/shard_map/ppermute | solution.py:189
  11.2 15.1 %collective-permute-start.1 = (bf16[26,64,128]{2,1,0:T(8,128)(2,1)}, bf16[26,64,128]{2,1,0:T(8,128)(2,1)S(1)}, u32[]{:S(2)}, u32[]{:S(2)}) collective-permute-start(bf16[26,64,128]{2,1,0:T(8,128)(2,1)} %get-tuple-element.17), channel_id=1, source_target_pairs={{0,12},{1,13},{2,14},{3,15},{4,0},{5,1},{6,2},{7,3},{8,4},{9,5},{1... | collective-permute-start | bytes 1277960 | tf_op jit(solution)/shard_map/ppermute | solution.py:166
  15.8 19.6 %collective-permute-start.2 = (bf16[26,64,128]{2,1,0:T(8,128)(2,1)}, bf16[26,64,128]{2,1,0:T(8,128)(2,1)S(1)}, u32[]{:S(2)}, u32[]{:S(2)}) collective-permute-start(bf16[26,64,128]{2,1,0:T(8,128)(2,1)} %get-tuple-element.18), channel_id=1, source_target_pairs={{0,13},{1,12},{2,15},{3,14},{4,1},{5,0},{6,3},{7,2},{8,5},{9,4},{1... | collective-permute-start | bytes 1277960 | tf_op jit(solution)/shard_map/ppermute | solution.py:166
  16.1 34.4 %collective-permute-start.3 = (bf16[26,64,128]{2,1,0:T(8,128)(2,1)}, bf16[26,64,128]{2,1,0:T(8,128)(2,1)S(1)}, u32[]{:S(2)}, u32[]{:S(2)}) collective-permute-start(bf16[26,64,128]{2,1,0:T(8,128)(2,1)} %get-tuple-element.19), channel_id=1, source_target_pairs={{0,12},{1,13},{2,14},{3,15},{4,0},{5,1},{6,2},{7,3},{8,4},{9,5},{1... | collective-permute-start | bytes 1277960 | tf_op jit(solution)/shard_map/ppermute | solution.py:166
  16.5 36.7 %collective-permute-start.4 = (bf16[26,64,128]{2,1,0:T(8,128)(2,1)}, bf16[26,64,128]{2,1,0:T(8,128)(2,1)S(1)}, u32[]{:S(2)}, u32[]{:S(2)}) collective-permute-start(bf16[26,64,128]{2,1,0:T(8,128)(2,1)} %get-tuple-element.20), channel_id=1, source_target_pairs={{0,13},{1,12},{2,15},{3,14},{4,1},{5,0},{6,3},{7,2},{8,5},{9,4},{1... | collective-permute-start | bytes 1277960 | tf_op jit(solution)/shard_map/ppermute | solution.py:166
  26.3 38.7 %collective-permute-start.7 = (bf16[26,64,128]{2,1,0:T(8,128)(2,1)S(1)}, bf16[26,64,128]{2,1,0:T(8,128)(2,1)S(1)}, u32[]{:S(2)}, u32[]{:S(2)}) collective-permute-start(bf16[26,64,128]{2,1,0:T(8,128)(2,1)S(1)} %broadcast_select_fusion.1), channel_id=1, source_target_pairs={{0,2},{1,3},{2,0},{3,1},{4,6},{5,7},{6,4},{7,5},{8,10},{9,11},{10,... | collective-permute-start | bytes 1277960 | tf_op jit(solution)/shard_map/ppermute | solution.py:181
  35.4 17.9 %copy-start.2 = (bf16[26,64,128]{2,1,0:T(8,128)(2,1)S(1)}, bf16[26,64,128]{2,1,0:T(8,128)(2,1)}, u32[]{:S(2)}) copy-start(bf16[26,64,128]{2,1,0:T(8,128)(2,1)} %get-tuple-element.19) | copy-start | bytes 1277956
  35.4 17.9 %copy-start.3 = (bf16[26,64,128]{2,1,0:T(8,128)(2,1)S(1)}, bf16[26,64,128]{2,1,0:T(8,128)(2,1)}, u32[]{:S(2)}) copy-start(bf16[26,64,128]{2,1,0:T(8,128)(2,1)} %get-tuple-element.20) | copy-start | bytes 1277956
  35.4 29.6 %collective-permute-start.8 = (bf16[26,64,128]{2,1,0:T(8,128)(2,1)S(1)}, bf16[26,64,128]{2,1,0:T(8,128)(2,1)S(1)}, u32[]{:S(2)}, u32[]{:S(2)}) collective-permute-start(bf16[26,64,128]{2,1,0:T(8,128)(2,1)S(1)} %broadcast_select_fusion), channel_id=1, source_target_pairs={{0,2},{1,3},{2,1},{3,0},{4,6},{5,7},{6,5},{7,4},{8,10},{9,11},{10,... | collective-permute-start | bytes 1277960 | tf_op jit(solution)/shard_map/ppermute | solution.py:181
  38.1 1.6 %copy-start = (bf16[64,128,128]{2,1,0:T(8,128)(2,1)S(1)}, bf16[64,128,128]{2,1,0:T(8,128)(2,1)}, u32[]{:S(2)}) copy-start(bf16[64,128,128]{2,1,0:T(8,128)(2,1)} %get-tuple-element.16.own_ref) | copy-start | bytes 6291460
  39.7 1.2 %copy-start.1 = (bf16[1024,512]{1,0:T(8,128)(2,1)S(1)}, bf16[1024,512]{1,0:T(8,128)(2,1)}, u32[]{:S(2)}) copy-start(bf16[1024,512]{1,0:T(8,128)(2,1)} %constant.34.clone.table_ref) | copy-start | bytes 3145732
  53.4 21.3 %collective-permute-start.5 = (bf16[26,64,128]{2,1,0:T(8,128)(2,1)S(1)}, bf16[26,64,128]{2,1,0:T(8,128)(2,1)S(1)}, u32[]{:S(2)}, u32[]{:S(2)}) collective-permute-start(bf16[26,64,128]{2,1,0:T(8,128)(2,1)S(1)} %get-tuple-element.24), channel_id=1, source_target_pairs={{0,2},{1,3},{2,0},{3,1},{4,6},{5,7},{6,4},{7,5},{8,10},{9,11},{10,... | collective-permute-start | bytes 1277960 | tf_op jit(solution)/shard_map/ppermute | solution.py:181
  54.9 19.7 %collective-permute-start.6 = (bf16[26,64,128]{2,1,0:T(8,128)(2,1)S(1)}, bf16[26,64,128]{2,1,0:T(8,128)(2,1)S(1)}, u32[]{:S(2)}, u32[]{:S(2)}) collective-permute-start(bf16[26,64,128]{2,1,0:T(8,128)(2,1)S(1)} %get-tuple-element.25), channel_id=1, source_target_pairs={{0,2},{1,3},{2,1},{3,0},{4,6},{5,7},{6,5},{7,4},{8,10},{9,11},{10,... | collective-permute-start | bytes 1277960 | tf_op jit(solution)/shard_map/ppermute | solution.py:181
